TPU v7x, 256 devices: a whole 4x4x8 slice. The times are simulated.
256 devices in a mesh: space: 16 (over z, y_hi), leaf: 16 (over x, y_lo, core).
Axes of the slice: x: 4, y: 4 (y_hi: 2, y_lo: 2; y = y_hi * 2 + y_lo), z: 8, core: 2. Of those that a mesh axis runs over, the one named last changes fastest.
Arguments:
- charges: bfloat16 [16, 2097152], P(None, ('space', 'leaf')), may hold values from -6 to 6
- leaf_basis: bfloat16 [16384, 64, 128], P(('space', 'leaf')), may hold values from -0.5 to 0.5
- transfer_one: bfloat16 [2048, 64, 512], P(('space', 'leaf')), may hold values from -0.25 to 0.25
- transfer_two: bfloat16 [256, 64, 512], P(('space', 'leaf')), may hold values from -0.25 to 0.25
- nodes_leaf: bfloat16 [16384, 3, 64], P(('space', 'leaf')), may hold values from 0 to 6
- nodes_one: bfloat16 [2048, 3, 64], P(('space', 'leaf')), may hold values from 0 to 6
- nodes_two: bfloat16 [256, 3, 64], P(('space', 'leaf')), may hold values from 0 to 6
- links_leaf: int32 [16384, 96], P(('space', 'leaf')), may hold values from -1 to 16383, as said below
- links_one: int32 [2048, 96], P(('space', 'leaf')), may hold values from -1 to 2047, as said below
- links_two: int32 [256, 96], P(('space', 'leaf')), may hold values from -1 to 255, as said below
Outputs:
- potentials: bfloat16 [16, 2097152], P(None, ('space', 'leaf'))
Inputs may be any that keep to these rules, and one draw needn't show every extreme that they name: `links_leaf`: A live source leaf lies on a device whose space index differs from that of the target leaf's device by at most one; live slots of a row come first. `links_one`: A live source cluster lies on a device whose space index differs from that of the target's device by at most one; live slots of a row come first. `links_two`: live slots of a row come first.
All inputs are finite; a program needn't handle non-finite values.
Results may differ from a plain program's by a relative error of at most 0.007.
Values may be sent and summed in bfloat16 or wider, within the bound.
A program may use at most 128 MiB of HBM per device.

v0:
```python
import jax
import jax.numpy as jnp
from jax import lax
from jax.sharding import PartitionSpec as P

SQRT_THREE = 1.7320508075688772
LENGTH = 2.0
AMPLITUDE = 0.25


def with_halo(cells, sides, width):
    for axis, dim in sides:
        count = lax.axis_size(axis)
        ends = count - 1
        head = lax.slice_in_dim(cells, 0, width, axis=dim)
        tail = lax.slice_in_dim(cells, cells.shape[dim] - width, cells.shape[dim], axis=dim)
        cells = jnp.concatenate(
            [
                lax.ppermute(tail, axis, [(i, (i + 1) % count) for i in range(ends)]),
                cells,
                lax.ppermute(head, axis, [((i + 1) % count, i) for i in range(ends)]),
            ],
            axis=dim,
        )
    return cells


def matern_block(target_nodes, source_nodes):
    diff = target_nodes[:, None, :, :, None] - source_nodes[:, :, :, None, :]
    dist = jnp.sqrt(jnp.sum(diff * diff, axis=2)) * (SQRT_THREE / LENGTH)
    return (AMPLITUDE * (1.0 + dist) * jnp.exp(-dist)).astype(jnp.bfloat16)


def couple(table_coef, table_nodes, rows, live, target_nodes, rank, width):
    count = rows.shape[0]
    slots = rows.shape[1]
    group = min(count, 4)

    def one_group(args):
        index, alive, tnodes = args
        picked = table_coef[index].reshape(group, slots, rank, width)
        picked = jnp.where(alive[:, :, None, None], picked, jnp.zeros((), jnp.bfloat16))
        source_nodes = table_nodes[index].astype(jnp.float32)
        matrix = matern_block(tnodes.astype(jnp.float32), source_nodes)
        return jnp.einsum("gjab,gjbv->gav", matrix, picked, preferred_element_type=jnp.float32)

    result = lax.map(
        one_group,
        (
            rows.reshape(-1, group, slots),
            live.reshape(-1, group, slots),
            target_nodes.reshape(-1, group, 3, rank),
        ),
    )
    return result.reshape(count, rank, width)


def local(
    charges,
    leaf_basis,
    transfer_one,
    transfer_two,
    nodes_leaf,
    nodes_one,
    nodes_two,
    links_leaf,
    links_one,
    links_two,
):
    width = charges.shape[0]
    leaf_dev = leaf_basis.shape[0]
    rank = leaf_basis.shape[1]
    leaf_size = leaf_basis.shape[2]
    one_dev = leaf_dev // 8
    two_dev = one_dev // 8
    n_leaf = lax.axis_size("leaf")
    my_space = lax.axis_index("space")
    shaped = charges.reshape(width, leaf_dev, leaf_size)
    coef_leaf = jnp.einsum(
        "tkp,vtp->tkv", leaf_basis, shaped, preferred_element_type=jnp.float32
    ).astype(jnp.bfloat16)
    coef_one = jnp.einsum(
        "pkm,pmv->pkv",
        transfer_one,
        coef_leaf.reshape(one_dev, 8 * rank, width),
        preferred_element_type=jnp.float32,
    ).astype(jnp.bfloat16)
    coef_two = jnp.einsum(
        "pkm,pmv->pkv",
        transfer_two,
        coef_one.reshape(two_dev, 8 * rank, width),
        preferred_element_type=jnp.float32,
    ).astype(jnp.bfloat16)
    flat_leaf = coef_leaf.reshape(leaf_dev, rank * width)
    whole_coef, whole_nodes = (
        lax.all_gather(flat_leaf, "leaf", axis=0, tiled=True),
        lax.all_gather(nodes_leaf, "leaf", axis=0, tiled=True),
    )
    near_coef, near_nodes = (
        with_halo(whole_coef[None], (("space", 0),), 1),
        with_halo(whole_nodes[None], (("space", 0),), 1),
    )
    live_leaf = links_leaf >= 0
    safe_leaf = jnp.where(live_leaf, links_leaf, 0)
    owner = safe_leaf // leaf_dev
    rows_leaf = (
        (owner // n_leaf - my_space + 1) * (n_leaf * leaf_dev)
        + owner % n_leaf * leaf_dev
        + safe_leaf % leaf_dev
    )
    rows_leaf = jnp.where(live_leaf, rows_leaf, 0)
    far_leaf = couple(
        near_coef.reshape(-1, rank * width),
        near_nodes.reshape(-1, 3, rank),
        rows_leaf,
        live_leaf,
        nodes_leaf,
        rank,
        width,
    )
    flat_one = coef_one.reshape(one_dev, rank * width)
    block_coef, block_nodes = (
        lax.all_gather(flat_one, "leaf", axis=0, tiled=True),
        lax.all_gather(nodes_one, "leaf", axis=0, tiled=True),
    )
    band_coef, band_nodes = (
        with_halo(block_coef[None], (("space", 0),), 1),
        with_halo(block_nodes[None], (("space", 0),), 1),
    )
    live_one = links_one >= 0
    safe_one = jnp.where(live_one, links_one, 0)
    owner_one = safe_one // one_dev
    rows_one = (
        (owner_one // n_leaf - my_space + 1) * (n_leaf * one_dev)
        + owner_one % n_leaf * one_dev
        + safe_one % one_dev
    )
    rows_one = jnp.where(live_one, rows_one, 0)
    far_one = couple(
        band_coef.reshape(-1, rank * width),
        band_nodes.reshape(-1, 3, rank),
        rows_one,
        live_one,
        nodes_one,
        rank,
        width,
    )
    flat_two = coef_two.reshape(two_dev, rank * width)
    every_coef, every_nodes = (
        lax.all_gather(flat_two, ("space", "leaf"), axis=0, tiled=True),
        lax.all_gather(nodes_two, ("space", "leaf"), axis=0, tiled=True),
    )
    live_two = links_two >= 0
    rows_two = jnp.where(live_two, links_two, 0)
    far_two = couple(every_coef, every_nodes, rows_two, live_two, nodes_two, rank, width)
    local_two = far_two.astype(jnp.bfloat16)
    down_one = jnp.einsum(
        "pkm,pkv->pmv", transfer_two, local_two, preferred_element_type=jnp.float32
    )
    local_one = (far_one + down_one.reshape(one_dev, rank, width)).astype(jnp.bfloat16)
    down_leaf = jnp.einsum(
        "pkm,pkv->pmv", transfer_one, local_one, preferred_element_type=jnp.float32
    )
    local_leaf = (far_leaf + down_leaf.reshape(leaf_dev, rank, width)).astype(jnp.bfloat16)
    result = jnp.einsum("tkp,tkv->vtp", leaf_basis, local_leaf, preferred_element_type=jnp.float32)
    return result.reshape(width, leaf_dev * leaf_size).astype(jnp.bfloat16)


def solution(mesh):
    return jax.shard_map(
        local,
        mesh=mesh,
        in_specs=(
            P(None, ("space", "leaf")),
            P(("space", "leaf"), None, None),
            P(("space", "leaf"), None, None),
            P(("space", "leaf"), None, None),
            P(("space", "leaf"), None, None),
            P(("space", "leaf"), None, None),
            P(("space", "leaf"), None, None),
            P(("space", "leaf"), None),
            P(("space", "leaf"), None),
            P(("space", "leaf"), None),
        ),
        out_specs=P(None, ("space", "leaf")),
        check_vma=False,
    )
```

profile of v0, /device:TPU:137, one launch (start us, length us, event | category | flops | bytes accessed | tf_op | source)
XLA Modules:
  0.0 1369.0 jit_solution(4095242045511093542)
XLA Ops:
  10.6 17.4 %all_gather.20 = bf16[128,3,64]{2,0,1:T(8,128)(2,1)S(1)} all-gather(bf16[8,3,64]{2,0,1:T(8,128)(2,1)} %param.19), channel_id=1, replica_groups=mesh['space'=16,'leaf'=16] {'leaf'}, dimensions={0}, use_global_device_ids=true | all-gather | bytes 52224 | tf_op jit(solution)/shard_map/all_gather | solution.py:124
  36.7 21.0 %all_gather.21 = bf16[128,1024]{1,0:T(8,128)(2,1)S(1)} all-gather(bf16[8,1024]{1,0:T(8,128)(2,1)S(1)} %reshape.238), channel_id=1, replica_groups=mesh['space'=16,'leaf'=16] {'leaf'}, dimensions={0}, use_global_device_ids=true | all-gather | bytes 278528 | tf_op jit(solution)/shard_map/all_gather | solution.py:123
  57.7 5.6 collective-permute-start.7
  66.1 26.5 %all_gather.18 = bf16[1024,3,64]{2,1,0:T(4,128)(2,1)S(1)} all-gather(bf16[64,3,64]{2,1,0:T(4,128)(2,1)S(1)} %copy.244), channel_id=1, replica_groups=mesh['space'=16,'leaf'=16] {'leaf'}, dimensions={0}, use_global_device_ids=true | all-gather | bytes 417792 | tf_op jit(solution)/shard_map/all_gather | solution.py:97
  95.8 340.5 %all_gather.22 = bf16[256,3,64]{2,1,0:T(4,128)(2,1)S(1)} all-gather(bf16[1,3,64]{2,1,0:T(4,128)(2,1)S(1)} %copy-done.10), channel_id=1, replica_groups=mesh['space'=16,'leaf'=16] {'space','leaf'}, dimensions={0}, use_global_device_ids=true | all-gather | bytes 98688 | tf_op jit(solution)/shard_map/all_gather | solution.py:151
  437.6 349.1 %all-gather = bf16[256,1,1024]{2,1,0:T(2,128)(2,1)S(1)} all-gather(bf16[1,1,1024]{2,1,0:T(2,128)(2,1)S(1)} %reshape.311), channel_id=1, replica_groups=mesh['space'=16,'leaf'=16] {'space','leaf'}, dimensions={0}, use_global_device_ids=true | all-gather | bytes 526336 | tf_op jit(solution)/shard_map/all_gather | solution.py:150
  797.6 7.0 collective-permute-start.3
  806.5 70.0 %while.25 = (s32[]{:T(128)}, f32[2,4,64,16]{2,3,1,0:T(8,128)}, bf16[2,4,3,64]{3,2,1,0:T(4,128)(2,1)S(1)}, s32[2,4,96]{2,1,0:T(4,128)S(1)}, bf16[384,3,64]{2,1,0:...) while((s32[]{:T(128)}, f32[2,4,64,16]{2,3,1,0:T(8,128)}, ...), condition=%wide.region_5.6_spmd, body=%wide.region_3.5_spmd.sunk | while | flops 72747904 | bytes 27565348 | solution.py:47
  819.4 6.5 multiply_reduce_fusion.6
  825.9 7.7 multiply_convert_fusion.6
  840.4 5.7 fusion.78
  849.1 6.5 multiply_reduce_fusion.6
  855.6 7.7 multiply_convert_fusion.6
  870.1 5.7 fusion.78
  887.6 12.3 collective-permute-done.3
  900.0 5.5 pad_maximum_fusion
  905.5 453.9 %while.24 = (s32[]{:T(128)}, f32[16,4,64,16]{2,1,0,3:T(4,128)}, bf16[16,4,3,64]{3,2,1,0:T(4,128)(2,1)S(1)}, s32[16,4,96]{2,1,0:T(4,128)}, bf16[3072,3,64]{2,1,0:...) while((s32[]{:T(128)}, f32[16,4,64,16]{2,1,0,3:T(4,128)}, ...), condition=%wide.region_2.3_spmd, body=%wide.region_0.2_spmd.sunk | while | flops 72747904 | bytes 27270436 | solution.py:47
  913.6 5.4 multiply_convert_fusion.5
  919.0 6.4 gather_fusion.1
  927.5 5.7 fusion.75
  942.0 5.4 multiply_convert_fusion.5
  947.4 6.4 gather_fusion.1
  955.8 5.7 fusion.75
  970.3 5.4 multiply_convert_fusion.5
  975.8 6.4 gather_fusion.1
  984.3 5.7 fusion.75
  998.8 5.4 multiply_convert_fusion.5
  1004.2 6.4 gather_fusion.1
  1012.6 5.7 fusion.75
  1027.1 5.4 multiply_convert_fusion.5
  1032.6 6.4 gather_fusion.1
  1041.0 5.7 fusion.75
  1055.5 5.4 multiply_convert_fusion.5
  1061.0 6.4 gather_fusion.1
  1069.4 5.7 fusion.75
  1083.9 5.4 multiply_convert_fusion.5
  1089.3 6.4 gather_fusion.1
  1097.7 5.7 fusion.75
  1112.2 5.4 multiply_convert_fusion.5
  1117.6 6.4 gather_fusion.1
  1126.1 5.7 fusion.75
  1140.6 5.4 multiply_convert_fusion.5
  1146.0 6.4 gather_fusion.1
  1154.5 5.7 fusion.75
  1174.4 6.4 gather_fusion.1
  1182.8 5.7 fusion.75
  1197.3 5.4 multiply_convert_fusion.5
  1202.8 6.4 gather_fusion.1
  1211.2 5.7 fusion.75
  1225.7 5.4 multiply_convert_fusion.5
  1231.1 6.4 gather_fusion.1
  1239.5 5.7 fusion.75
  1254.0 5.4 multiply_convert_fusion.5
  1259.5 6.4 gather_fusion.1
  1267.9 5.7 fusion.75
  1282.3 5.4 multiply_convert_fusion.5
  1287.8 6.4 gather_fusion.1
  1296.3 5.7 fusion.75
  1310.8 5.4 multiply_convert_fusion.5
  1316.2 6.4 gather_fusion.1
  1324.7 5.7 fusion.75
  1339.2 5.4 multiply_convert_fusion.5
  1344.6 6.4 gather_fusion.1
  1353.0 5.7 fusion.75
  (367 shorter events, 243.1 us)
Async XLA Ops:
  6.5 1.2 copy-start
  6.5 89.3 %copy-start.10 = (bf16[1,3,64]{2,1,0:T(4,128)(2,1)S(1)}, bf16[1,3,64]{2,1,0:T(4,128)(2,1)}, u32[]{:S(2)}) copy-start(bf16[1,3,64]{2,1,0:T(4,128)(2,1)} %param.20) | copy-start | bytes 1156
  6.5 429.8 %copy-start.11 = (s32[1,96]{1,0:T(1,128)S(1)}, s32[1,96]{1,0:T(1,128)}, u32[]{:S(2)}) copy-start(s32[1,96]{1,0:T(1,128)} %param.23) | copy-start | bytes 1156
  6.5 430.7 %copy-start.5 = (bf16[1,64,512]{2,1,0:T(8,128)(2,1)S(1)}, bf16[1,64,512]{2,1,0:T(8,128)(2,1)}, u32[]{:S(2)}) copy-start(bf16[1,64,512]{2,1,0:T(8,128)(2,1)} %param.17) | copy-start | bytes 196612
  6.5 791.0 %all-gather.3.cloned.1.call-start = ((), (), s32[]{:S(2)}) async-start(), calls=%async_computation | async-start | bytes 2228224 | tf_op jit(solution)/shard_map/all_gather | solution.py:96
  9.3 778.5 %copy-start.9 = (s32[8,96]{1,0:T(8,128)S(1)}, s32[8,96]{1,0:T(8,128)}, u32[]{:S(2)}) copy-start(s32[8,96]{1,0:T(8,128)} %param.22) | copy-start | bytes 9220
  9.3 779.1 %copy-start.6 = (s32[64,96]{1,0:T(8,128)S(1)}, s32[64,96]{1,0:T(8,128)}, u32[]{:S(2)}) copy-start(s32[64,96]{1,0:T(8,128)} %param.21) | copy-start | bytes 73732
  28.0 765.2 %collective-permute-start.5 = (bf16[1,128,3,64]{3,1,2,0:T(8,128)(2,1)S(1)}, bf16[1,128,3,64]{3,1,2,0:T(8,128)(2,1)}, u32[]{:S(2)}, u32[]{:S(2)}) collective-permute-start(bf16[1,128,3,64]{3,1,2,0:T(8,128)(2,1)S(1)} %bitcast.156), channel_id=1, source_target_pairs={{16,0},{32,16},{48,32},{64,48},{80,64},{96,80},{112,96},{128,112},... | collective-permute-start | bytes 147464 | tf_op jit(solution)/shard_map/ppermute | solution.py:21
  31.8 763.3 %collective-permute-start.4 = (bf16[1,128,3,64]{3,1,2,0:T(8,128)(2,1)S(1)}, bf16[1,128,3,64]{3,1,2,0:T(8,128)(2,1)}, u32[]{:S(2)}, u32[]{:S(2)}) collective-permute-start(bf16[1,128,3,64]{3,1,2,0:T(8,128)(2,1)S(1)} %bitcast.157), channel_id=1, source_target_pairs={{0,16},{16,32},{32,48},{48,64},{64,80},{80,96},{96,112},{112,128},... | collective-permute-start | bytes 147464 | tf_op jit(solution)/shard_map/ppermute | solution.py:19
  57.7 738.7 %collective-permute-start.7 = (bf16[1,128,1024]{2,1,0:T(8,128)(2,1)S(1)}, bf16[1,128,1024]{2,1,0:T(8,128)(2,1)}, u32[]{:S(2)}, u32[]{:S(2)}) collective-permute-start(bf16[1,128,1024]{2,1,0:T(8,128)(2,1)S(1)} %bitcast.151), channel_id=1, source_target_pairs={{16,0},{32,16},{48,32},{64,48},{80,64},{96,80},{112,96},{128,112},... | collective-permute-start | bytes 786440 | tf_op jit(solution)/shard_map/ppermute | solution.py:21
  63.3 733.1 %collective-permute-start.6 = (bf16[1,128,1024]{2,1,0:T(8,128)(2,1)S(1)}, bf16[1,128,1024]{2,1,0:T(8,128)(2,1)}, u32[]{:S(2)}, u32[]{:S(2)}) collective-permute-start(bf16[1,128,1024]{2,1,0:T(8,128)(2,1)S(1)} %bitcast.152), channel_id=1, source_target_pairs={{0,16},{16,32},{32,48},{48,64},{64,80},{80,96},{96,112},{112,128},... | collective-permute-start | bytes 786440 | tf_op jit(solution)/shard_map/ppermute | solution.py:19
  92.6 699.0 %copy-start.1 = (bf16[1024,3,64]{2,1,0:T(4,128)(2,1)}, bf16[1024,3,64]{2,1,0:T(4,128)(2,1)S(1)}, u32[]{:S(2)}) copy-start(bf16[1024,3,64]{2,1,0:T(4,128)(2,1)S(1)} %all_gather.18) | copy-start | bytes 1179652
  93.8 785.2 %collective-permute-start.1 = (bf16[1,1024,3,64]{1,3,2,0:T(8,128)(2,1)}, bf16[1,1024,3,64]{1,3,2,0:T(8,128)(2,1)}, u32[]{:S(2)}, u32[]{:S(2)}) collective-permute-start(bf16[1,1024,3,64]{1,3,2,0:T(8,128)(2,1)} %copy.246), channel_id=1, source_target_pairs={{16,0},{32,16},{48,32},{64,48},{80,64},{96,80},{112,96},{128,112},... | collective-permute-start | bytes 1179656 | tf_op jit(solution)/shard_map/ppermute | solution.py:21
  793.2 87.4 %collective-permute-start = (bf16[1,1024,3,64]{1,3,2,0:T(8,128)(2,1)}, bf16[1,1024,3,64]{1,3,2,0:T(8,128)(2,1)}, u32[]{:S(2)}, u32[]{:S(2)}) collective-permute-start(bf16[1,1024,3,64]{1,3,2,0:T(8,128)(2,1)} %copy.246), channel_id=1, source_target_pairs={{0,16},{16,32},{32,48},{48,64},{64,80},{80,96},{96,112},{112,128},... | collective-permute-start | bytes 1179656 | tf_op jit(solution)/shard_map/ppermute | solution.py:19
  797.6 102.4 %collective-permute-start.3 = (bf16[1,1024,1024]{2,1,0:T(8,128)(2,1)}, bf16[1,1024,1024]{2,1,0:T(8,128)(2,1)}, u32[]{:S(2)}, u32[]{:S(2)}) collective-permute-start(bf16[1,1024,1024]{2,1,0:T(8,128)(2,1)} %bitcast.147), channel_id=1, source_target_pairs={{16,0},{32,16},{48,32},{64,48},{80,64},{96,80},{112,96},{128,112},... | collective-permute-start | bytes 6291464 | tf_op jit(solution)/shard_map/ppermute | solution.py:21
  804.5 95.4 %collective-permute-start.2 = (bf16[1,1024,1024]{2,1,0:T(8,128)(2,1)}, bf16[1,1024,1024]{2,1,0:T(8,128)(2,1)}, u32[]{:S(2)}, u32[]{:S(2)}) collective-permute-start(bf16[1,1024,1024]{2,1,0:T(8,128)(2,1)} %bitcast.148), channel_id=1, source_target_pairs={{0,16},{16,32},{32,48},{48,64},{64,80},{80,96},{96,112},{112,128},... | collective-permute-start | bytes 6291464 | tf_op jit(solution)/shard_map/ppermute | solution.py:19
  833.6 6.8 copy-start.7
  846.2 0.6 copy-start.8
  863.3 6.8 copy-start.7
  875.9 0.6 copy-start.8
  882.2 17.7 %copy-start.2 = (bf16[1024,1024]{1,0:T(8,128)(2,1)S(1)}, bf16[1024,1024]{1,0:T(8,128)(2,1)}, u32[]{:S(2)}) copy-start(bf16[1024,1024]{1,0:T(8,128)(2,1)} %all-gather.3.cloned.1.call-done) | copy-start | bytes 6291460
  905.5 3.9 copy-start.3
  925.4 8.4 copy-start.4
  933.8 3.9 copy-start.3
  953.8 8.5 copy-start.4
  962.2 3.9 copy-start.3
  982.2 8.5 copy-start.4
  990.6 3.9 copy-start.3
  1010.6 8.4 copy-start.4
  1019.0 3.9 copy-start.3
  1038.9 8.5 copy-start.4
  1047.4 3.9 copy-start.3
  1067.3 8.4 copy-start.4
  1075.7 3.9 copy-start.3
  1095.7 8.4 copy-start.4
  1104.1 3.9 copy-start.3
  1124.0 8.5 copy-start.4
  1132.5 3.9 copy-start.3
  1152.4 8.5 copy-start.4
  1160.9 3.9 copy-start.3
  1180.8 8.4 copy-start.4
  1189.2 3.9 copy-start.3
  1209.1 8.4 copy-start.4
  1217.5 3.9 copy-start.3
  1237.5 8.4 copy-start.4
  1245.9 3.9 copy-start.3
  1265.8 8.4 copy-start.4
  1274.2 3.9 copy-start.3
  1294.1 8.5 copy-start.4
  1302.7 3.9 copy-start.3
  1322.6 8.5 copy-start.4
  1331.1 3.9 copy-start.3
  1351.0 8.4 copy-start.4
Sparse Core Ops, SparseCore 0:
  10.7 40.2 all-gather.2
where the time goes:
time: 1380 us; the launch traced here: 1370 us
  blocking collectives  755 us (55%)
  local copies, waits for them, and re-layouts  224 us (16%)
  other arithmetic  216 us (16%)
  matrix products  109 us (8%)
  starting transfers between devices  27 us (2%)
  between operations  14.1 us (1%)
    all_gather x1, blocking collectives, local(): lax.all_gather(flat_two, ('space', 'leaf'), axis=0, tiled=True)  349 us
    all_gather x1, blocking collectives, local(): lax.all_gather(nodes_two, ('space', 'leaf'), axis=0, tiled=True)  341 us
    gather x38, local copies, waits for them, and re-layouts, one_group(): picked = table_coef[index].reshape(group, slots, rank, width)  115 us
    dot_general x19, matrix products, one_group(): jnp.einsum('gjab,gjbv->gav', matrix, picked, preferred_element_type=jnp.f...  104 us
    convert_element_type x19, other arithmetic, matern_block(): return (AMPLITUDE * (1.0 + dist) * jnp.exp(-dist)).astype(jnp.bfloat16)  103 us
    reduce_sum x19, other arithmetic, matern_block(): dist = jnp.sqrt(jnp.sum(diff * diff, axis=2)) * (SQRT_THREE / LENGTH)  66.6 us
    gather x20, local copies, waits for them, and re-layouts, one_group(): source_nodes = table_nodes[index].astype(jnp.float32)  54.8 us
  transfers between devices with their start and end apart: 9, of which 1 were waited for; matrix products, arithmetic and copies ran while one was open for 6% of the time, Pallas kernels for 0%

commit v1 on v0

--- a/solution.py
+++ b/solution.py
@@ -147,7 +147,15 @@
     )
     flat_two = coef_two.reshape(two_dev, rank * width)
     every_coef, every_nodes = (
-        lax.all_gather(flat_two, ("space", "leaf"), axis=0, tiled=True),
+        jnp.concatenate(
+            lax.all_to_all(
+                jnp.stack([flat_two for _ in range(lax.axis_size(("space", "leaf")))]),
+                ("space", "leaf"),
+                0,
+                0,
+            ),
+            axis=0,
+        ),
         lax.all_gather(nodes_two, ("space", "leaf"), axis=0, tiled=True),
     )
     live_two = links_two >= 0

time: 1380 us -> 1070 us (0.78)
  blocking collectives: 755 us -> 417 us
  starting transfers between devices: 27 us -> 41.7 us
    all_gather x1 -> x0, blocking collectives: 349 us -> none  [local(): lax.all_gather(flat_two, ('space', 'leaf'), axis=0, tiled=True)]
    all_to_all x0 -> x1, starting transfers between devices: none -> 14.6 us  [local(): lax.all_to_all(jnp.stack([flat_two for _ in range(lax.axis_size(('space',...]
  transfers between devices with their start and end apart: 9 -> 10, of which waited for: 1 -> 1; matrix products, arithmetic and copies ran while one was open for 6% -> 9% of each run, Pallas kernels for 0% -> 0%
where the time goes in v1:
time: 1070 us; the launch traced here: 1060 us
  blocking collectives  417 us (39%)
  local copies, waits for them, and re-layouts  231 us (22%)
  other arithmetic  225 us (21%)
  matrix products  109 us (10%)
  starting transfers between devices  41.7 us (4%)
  waiting for transfers between devices  18.8 us (2%)
  between operations  13.9 us (1%)
    all_gather x1, blocking collectives, local(): lax.all_gather(nodes_two, ('space', 'leaf'), axis=0, tiled=True)  352 us
    gather x38, local copies, waits for them, and re-layouts, one_group(): picked = table_coef[index].reshape(group, slots, rank, width)  115 us
    dot_general x19, matrix products, one_group(): jnp.einsum('gjab,gjbv->gav', matrix, picked, preferred_element_type=jnp.f...  105 us
    convert_element_type x19, other arithmetic, matern_block(): return (AMPLITUDE * (1.0 + dist) * jnp.exp(-dist)).astype(jnp.bfloat16)  104 us
    reduce_sum x19, other arithmetic, matern_block(): dist = jnp.sqrt(jnp.sum(diff * diff, axis=2)) * (SQRT_THREE / LENGTH)  66.6 us
    gather x20, local copies, waits for them, and re-layouts, one_group(): source_nodes = table_nodes[index].astype(jnp.float32)  54.8 us
    all_gather x1, blocking collectives, local(): lax.all_gather(nodes_leaf, 'leaf', axis=0, tiled=True)  25.9 us
  transfers between devices with their start and end apart: 10, of which 1 were waited for; matrix products, arithmetic and copies ran while one was open for 9% of the time, Pallas kernels for 0%

profile of v1, /device:TPU:137, one launch (start us, length us, event | category | flops | bytes accessed | tf_op | source)
XLA Modules:
  0.0 1056.7 jit_solution(5471091866150547112)
XLA Ops:
  10.6 17.4 %all_gather.17 = bf16[128,3,64]{2,0,1:T(8,128)(2,1)S(1)} all-gather(bf16[8,3,64]{2,0,1:T(8,128)(2,1)} %param.19), channel_id=1, replica_groups=mesh['space'=16,'leaf'=16] {'leaf'}, dimensions={0}, use_global_device_ids=true | all-gather | bytes 52224 | tf_op jit(solution)/shard_map/all_gather | solution.py:124
  36.7 21.0 %all_gather.18 = bf16[128,1024]{1,0:T(8,128)(2,1)S(1)} all-gather(bf16[8,1024]{1,0:T(8,128)(2,1)S(1)} %reshape.242), channel_id=1, replica_groups=mesh['space'=16,'leaf'=16] {'leaf'}, dimensions={0}, use_global_device_ids=true | all-gather | bytes 278528 | tf_op jit(solution)/shard_map/all_gather | solution.py:123
  57.7 5.6 collective-permute-start.7
  66.7 25.9 %all_gather.15 = bf16[1024,3,64]{2,1,0:T(4,128)(2,1)S(1)} all-gather(bf16[64,3,64]{2,1,0:T(4,128)(2,1)} %copy.242), channel_id=1, replica_groups=mesh['space'=16,'leaf'=16] {'leaf'}, dimensions={0}, use_global_device_ids=true | all-gather | bytes 417792 | tf_op jit(solution)/shard_map/all_gather | solution.py:97
  104.1 14.6 %all-to-all-start = ((bf16[256,2,512]{2,1,0:T(2,128)(2,1)}), bf16[256,2,512]{2,1,0:T(2,128)(2,1)}, u32[]{:S(2)}, u32[]{:S(2)}) async-start(bf16[256,2,512]{2,1,0:T(2,128)(2,1)} %reshape.319), calls=%async_computation | async-start | bytes 1048576 | tf_op jit(solution)/shard_map/all_to_all | solution.py:151
  118.7 352.3 %all_gather.19 = bf16[256,3,64]{2,1,0:T(4,128)(2,1)S(1)} all-gather(bf16[1,3,64]{2,1,0:T(4,128)(2,1)S(1)} %copy-done.10), channel_id=1, replica_groups=mesh['space'=16,'leaf'=16] {'space','leaf'}, dimensions={0}, use_global_device_ids=true | all-gather | bytes 98688 | tf_op jit(solution)/shard_map/all_gather | solution.py:159
  485.2 7.0 collective-permute-start.3
  494.2 58.0 %while.25 = (s32[]{:T(128)}, f32[2,4,64,16]{2,3,1,0:T(8,128)}, bf16[2,4,3,64]{3,2,1,0:T(4,128)(2,1)S(1)}, s32[2,4,96]{2,1,0:T(4,128)S(1)}, bf16[384,3,64]{2,1,0:...) while((s32[]{:T(128)}, f32[2,4,64,16]{2,3,1,0:T(8,128)}, ...), condition=%wide.region_5.6_spmd, body=%wide.region_3.5_spmd.sunk | while | flops 72747904 | bytes 27568448 | solution.py:47
  496.5 6.5 multiply_reduce_fusion.6
  503.0 7.6 multiply_convert_fusion.6
  516.8 5.7 fusion.78
  525.5 6.5 multiply_reduce_fusion.6
  532.0 7.6 multiply_convert_fusion.6
  545.8 5.7 fusion.78
  568.9 18.8 %collective-permute-done.3 = bf16[1,1024,1024]{2,1,0:T(8,128)(2,1)} collective-permute-done((bf16[1,1024,1024]{2,1,0:T(8,128)(2,1)}, bf16[1,1024,1024]{2,1,0:T(8,128)(2,1)}, u32[]{:S(2)}, u32[]{:S(2)}) %collective-permute-start.3) | collective-permute-done | bytes 2097184 | tf_op jit(solution)/shard_map/ppermute | solution.py:21
  587.6 6.4 pad_maximum_fusion
  594.1 453.2 %while.24 = (s32[]{:T(128)}, f32[16,4,64,16]{2,1,0,3:T(4,128)}, bf16[16,4,3,64]{3,2,1,0:T(4,128)(2,1)}, s32[16,4,96]{2,1,0:T(4,128)}, bf16[3072,3,64]{2,1,0:T(4,...) while((s32[]{:T(128)}, f32[16,4,64,16]{2,1,0,3:T(4,128)}, ...), condition=%wide.region_2.3_spmd, body=%wide.region_0.2_spmd.sunk | while | flops 72747904 | bytes 27073772 | solution.py:47
  602.2 5.4 multiply_convert_fusion.5
  607.6 6.4 gather_fusion.1
  616.1 5.7 fusion.75
  630.5 5.4 multiply_convert_fusion.5
  636.0 6.4 gather_fusion.1
  644.4 5.7 fusion.75
  658.9 5.4 multiply_convert_fusion.5
  664.3 6.4 gather_fusion.1
  672.8 5.7 fusion.75
  687.2 5.4 multiply_convert_fusion.5
  692.7 6.4 gather_fusion.1
  701.0 5.7 fusion.75
  715.5 5.4 multiply_convert_fusion.5
  720.9 6.4 gather_fusion.1
  729.3 5.7 fusion.75
  743.8 5.4 multiply_convert_fusion.5
  749.2 6.4 gather_fusion.1
  757.6 5.7 fusion.75
  772.1 5.4 multiply_convert_fusion.5
  777.6 6.4 gather_fusion.1
  785.9 5.7 fusion.75
  800.4 5.4 multiply_convert_fusion.5
  805.8 6.4 gather_fusion.1
  814.3 5.7 fusion.75
  828.8 5.4 multiply_convert_fusion.5
  834.2 6.4 gather_fusion.1
  842.6 5.7 fusion.75
  857.1 5.4 multiply_convert_fusion.5
  862.5 6.4 gather_fusion.1
  870.9 5.7 fusion.75
  885.4 5.4 multiply_convert_fusion.5
  890.8 6.4 gather_fusion.1
  899.3 5.7 fusion.75
  913.7 5.4 multiply_convert_fusion.5
  919.2 6.4 gather_fusion.1
  927.7 5.7 fusion.75
  942.1 5.4 multiply_convert_fusion.5
  947.6 6.4 gather_fusion.1
  955.9 5.7 fusion.75
  970.4 5.4 multiply_convert_fusion.5
  975.8 6.4 gather_fusion.1
  984.3 5.7 fusion.75
  998.7 5.4 multiply_convert_fusion.5
  1004.2 6.4 gather_fusion.1
  1012.6 5.7 fusion.75
  1032.5 6.4 gather_fusion.1
  1040.9 5.7 fusion.75
  (319 shorter events, 258.0 us)
Async XLA Ops:
  6.5 1.2 copy-start
  6.5 89.4 %copy-start.4 = (bf16[1,64,512]{2,1,0:T(8,128)(2,1)S(1)}, bf16[1,64,512]{2,1,0:T(8,128)(2,1)}, u32[]{:S(2)}) copy-start(bf16[1,64,512]{2,1,0:T(8,128)(2,1)} %param.17) | copy-start | bytes 196612
  6.5 112.2 %copy-start.10 = (bf16[1,3,64]{2,1,0:T(4,128)(2,1)S(1)}, bf16[1,3,64]{2,1,0:T(4,128)(2,1)}, u32[]{:S(2)}) copy-start(bf16[1,3,64]{2,1,0:T(4,128)(2,1)} %param.20) | copy-start | bytes 1156
  6.5 464.5 %copy-start.12 = (s32[1,96]{1,0:T(1,128)S(1)}, s32[1,96]{1,0:T(1,128)}, u32[]{:S(2)}) copy-start(s32[1,96]{1,0:T(1,128)} %param.23) | copy-start | bytes 1156
  6.5 465.4 %copy-start.9 = (s32[8,96]{1,0:T(8,128)S(1)}, s32[8,96]{1,0:T(8,128)}, u32[]{:S(2)}) copy-start(s32[8,96]{1,0:T(8,128)} %param.22) | copy-start | bytes 9220
  6.5 478.7 %all-gather.2.cloned.1.call-start = ((), (), s32[]{:S(2)}) async-start(), calls=%async_computation.1 | async-start | bytes 2228224 | tf_op jit(solution)/shard_map/all_gather | solution.py:96
  28.0 452.9 %collective-permute-start.5 = (bf16[1,128,3,64]{3,1,2,0:T(8,128)(2,1)S(1)}, bf16[1,128,3,64]{3,1,2,0:T(8,128)(2,1)}, u32[]{:S(2)}, u32[]{:S(2)}) collective-permute-start(bf16[1,128,3,64]{3,1,2,0:T(8,128)(2,1)S(1)} %bitcast.156), channel_id=1, source_target_pairs={{16,0},{32,16},{48,32},{64,48},{80,64},{96,80},{112,96},{128,112},... | collective-permute-start | bytes 147464 | tf_op jit(solution)/shard_map/ppermute | solution.py:21
  31.8 451.0 %collective-permute-start.4 = (bf16[1,128,3,64]{3,1,2,0:T(8,128)(2,1)S(1)}, bf16[1,128,3,64]{3,1,2,0:T(8,128)(2,1)}, u32[]{:S(2)}, u32[]{:S(2)}) collective-permute-start(bf16[1,128,3,64]{3,1,2,0:T(8,128)(2,1)S(1)} %bitcast.157), channel_id=1, source_target_pairs={{0,16},{16,32},{32,48},{48,64},{64,80},{80,96},{96,112},{112,128},... | collective-permute-start | bytes 147464 | tf_op jit(solution)/shard_map/ppermute | solution.py:19
  57.7 426.3 %collective-permute-start.7 = (bf16[1,128,1024]{2,1,0:T(8,128)(2,1)S(1)}, bf16[1,128,1024]{2,1,0:T(8,128)(2,1)}, u32[]{:S(2)}, u32[]{:S(2)}) collective-permute-start(bf16[1,128,1024]{2,1,0:T(8,128)(2,1)S(1)} %bitcast.151), channel_id=1, source_target_pairs={{16,0},{32,16},{48,32},{64,48},{80,64},{96,80},{112,96},{128,112},... | collective-permute-start | bytes 786440 | tf_op jit(solution)/shard_map/ppermute | solution.py:21
  63.3 420.8 %collective-permute-start.6 = (bf16[1,128,1024]{2,1,0:T(8,128)(2,1)S(1)}, bf16[1,128,1024]{2,1,0:T(8,128)(2,1)}, u32[]{:S(2)}, u32[]{:S(2)}) collective-permute-start(bf16[1,128,1024]{2,1,0:T(8,128)(2,1)S(1)} %bitcast.152), channel_id=1, source_target_pairs={{0,16},{16,32},{32,48},{48,64},{64,80},{80,96},{96,112},{112,128},... | collective-permute-start | bytes 786440 | tf_op jit(solution)/shard_map/ppermute | solution.py:19
  92.6 385.6 %copy-start.1 = (bf16[1024,3,64]{2,1,0:T(4,128)(2,1)}, bf16[1024,3,64]{2,1,0:T(4,128)(2,1)S(1)}, u32[]{:S(2)}) copy-start(bf16[1024,3,64]{2,1,0:T(4,128)(2,1)S(1)} %all_gather.15) | copy-start | bytes 1179652
  93.8 458.3 %collective-permute-start.1 = (bf16[1,1024,3,64]{1,3,2,0:T(8,128)(2,1)}, bf16[1,1024,3,64]{1,3,2,0:T(8,128)(2,1)}, u32[]{:S(2)}, u32[]{:S(2)}) collective-permute-start(bf16[1,1024,3,64]{1,3,2,0:T(8,128)(2,1)} %copy.244), channel_id=1, source_target_pairs={{16,0},{32,16},{48,32},{64,48},{80,64},{96,80},{112,96},{128,112},... | collective-permute-start | bytes 1179656 | tf_op jit(solution)/shard_map/ppermute | solution.py:21
  101.9 378.3 %copy-start.5 = (bf16[1,64,512]{2,1,0:T(8,128)(2,1)S(1)}, bf16[1,64,512]{2,1,0:T(8,128)(2,1)}, u32[]{:S(2)}) copy-start(bf16[1,64,512]{2,1,0:T(8,128)(2,1)} %param.17) | copy-start | bytes 196612
  104.1 456.6 %all-to-all-start = ((bf16[256,2,512]{2,1,0:T(2,128)(2,1)}), bf16[256,2,512]{2,1,0:T(2,128)(2,1)}, u32[]{:S(2)}, u32[]{:S(2)}) async-start(bf16[256,2,512]{2,1,0:T(2,128)(2,1)} %reshape.319), calls=%async_computation | async-start | bytes 1048576 | tf_op jit(solution)/shard_map/all_to_all | solution.py:151
  480.9 72.9 %collective-permute-start = (bf16[1,1024,3,64]{1,3,2,0:T(8,128)(2,1)}, bf16[1,1024,3,64]{1,3,2,0:T(8,128)(2,1)}, u32[]{:S(2)}, u32[]{:S(2)}) collective-permute-start(bf16[1,1024,3,64]{1,3,2,0:T(8,128)(2,1)} %copy.244), channel_id=1, source_target_pairs={{0,16},{16,32},{32,48},{48,64},{64,80},{80,96},{96,112},{112,128},... | collective-permute-start | bytes 1179656 | tf_op jit(solution)/shard_map/ppermute | solution.py:19
  485.2 102.4 %collective-permute-start.3 = (bf16[1,1024,1024]{2,1,0:T(8,128)(2,1)}, bf16[1,1024,1024]{2,1,0:T(8,128)(2,1)}, u32[]{:S(2)}, u32[]{:S(2)}) collective-permute-start(bf16[1,1024,1024]{2,1,0:T(8,128)(2,1)} %bitcast.147), channel_id=1, source_target_pairs={{16,0},{32,16},{48,32},{64,48},{80,64},{96,80},{112,96},{128,112},... | collective-permute-start | bytes 6291464 | tf_op jit(solution)/shard_map/ppermute | solution.py:21
  492.2 95.4 %collective-permute-start.2 = (bf16[1,1024,1024]{2,1,0:T(8,128)(2,1)}, bf16[1,1024,1024]{2,1,0:T(8,128)(2,1)}, u32[]{:S(2)}, u32[]{:S(2)}) collective-permute-start(bf16[1,1024,1024]{2,1,0:T(8,128)(2,1)} %bitcast.148), channel_id=1, source_target_pairs={{0,16},{16,32},{32,48},{48,64},{64,80},{80,96},{96,112},{112,128},... | collective-permute-start | bytes 6291464 | tf_op jit(solution)/shard_map/ppermute | solution.py:19
  510.6 5.7 copy-start.11
  510.6 6.2 copy-start.6
  522.5 0.6 copy-start.7
  539.5 5.7 copy-start.11
  539.6 6.2 copy-start.6
  551.5 0.6 copy-start.7
  553.7 11.7 %copy-start.13 = (pred[96]{0:T(512)(128)(4,1)S(1)}, pred[96]{0:T(512)(128)(4,1)}, u32[]{:S(2)}) copy-start(pred[96]{0:T(512)(128)(4,1)} %compare_bitcast_fusion) | copy-start | bytes 292
  555.4 12.0 %copy-start.3 = (bf16[512,64]{1,0:T(8,128)(2,1)S(1)}, bf16[512,64]{1,0:T(8,128)(2,1)}, u32[]{:S(2)}) copy-start(bf16[512,64]{1,0:T(8,128)(2,1)} %copy.271) | copy-start | bytes 196612
  555.4 12.0 %copy-start.8 = (f32[2,4,64,16]{2,3,1,0:T(8,128)S(1)}, f32[2,4,64,16]{2,3,1,0:T(8,128)}, u32[]{:S(2)}) copy-start(f32[2,4,64,16]{2,3,1,0:T(8,128)} %get-tuple-element.101) | copy-start | bytes 98308
  560.7 6.7 copy-start.2
Sparse Core Ops, SparseCore 0:
  10.7 40.2 all-gather.1
